TPU v7x, 256 devices: a whole 4x4x8 slice. The times are simulated.
256 devices in a mesh: dp: 32 (over x, y, core), owner: 8 (over z).
Axes of the slice: x: 4, y: 4, z: 8, core: 2. Of those that a mesh axis runs over, the one named last changes fastest.
Arguments:
- momentum: float32 [192, 1024, 768], P(None, ('dp', 'owner')), may hold values from -6 to 6
- grad: bfloat16 [192, 1024, 768], P(None, ('dp', 'owner'))
- owner_table: int32 [192], replicated, may hold values from 0 to 255, as said below
Outputs:
- new_momentum: float32 [192, 1024, 768], P(None, ('dp', 'owner'))
- update: float32 [192, 1024, 768], P(None, ('dp', 'owner'))
- owned_update: bfloat16 [2, 256, 1024, 768], P(None, ('dp', 'owner'))
Inputs may be any that keep to these rules, and one draw needn't show every extreme that they name: `owner_table`: no device owns more than 2 matrices, and some device owns exactly 2.
All inputs are finite; a program needn't handle non-finite values.
Results may differ from a plain program's by a relative error of at most 0.0073.
Values may be sent and summed in bfloat16 or wider, within the bound.
No kernel may reach another device: no remote copies, remote signals or barrier semaphores. Data moves between devices by JAX's collectives and lax.ppermute only.
A program may use at most 64 MiB of HBM per device.

v0:
```python
import math

import jax
import jax.numpy as jnp
from jax import lax
from jax.sharding import PartitionSpec as P

R = 1024
ITERS = 2
CAP = 2


momentum_decay = 0.95
quintic_one = 3.4445
quintic_two = -4.775
quintic_three = 2.0315
norm_epsilon = 1e-07


def orthogonalize(matrix):
    values = matrix.astype(jnp.float32)
    frobenius = jnp.sqrt(jnp.sum(values * values))
    iterate = (values / (frobenius + norm_epsilon)).astype(jnp.bfloat16)
    for step in range(ITERS):
        gram = lax.dot_general(
            iterate, iterate, (((0,), (0,)), ((), ())), preferred_element_type=jnp.float32
        ).astype(jnp.bfloat16)
        square = jnp.dot(gram, gram, preferred_element_type=jnp.float32)
        poly = (quintic_two * gram.astype(jnp.float32) + quintic_three * square).astype(
            jnp.bfloat16
        )
        iterate = (
            quintic_one * iterate.astype(jnp.float32)
            + jnp.dot(iterate, poly, preferred_element_type=jnp.float32)
        ).astype(jnp.bfloat16)
    return iterate


def owner_rank(owner_table):
    total_mats = owner_table.shape[0]
    matching = owner_table[:, None] == owner_table[None, :]
    earlier = lax.broadcasted_iota(jnp.int32, (total_mats, total_mats), 1) < lax.broadcasted_iota(
        jnp.int32, (total_mats, total_mats), 0
    )
    return jnp.sum(jnp.logical_and(matching, earlier).astype(jnp.int32), axis=1)


def shards(momentum, grad, owner_table):
    dp_count = lax.axis_size("dp")
    owner_count = lax.axis_size("owner")
    device_count = dp_count * owner_count
    mat_count, row_count, col_count = momentum.shape
    slot_count = CAP
    update_scale = math.sqrt(R)
    grad_values = grad.astype(jnp.float32)
    new_momentum = momentum_decay * momentum + grad_values
    nesterov = (grad_values + momentum_decay * new_momentum).astype(jnp.bfloat16)
    rank = owner_rank(owner_table)
    slot_index = rank * device_count + owner_table
    selector = (
        slot_index[None, :]
        == lax.broadcasted_iota(jnp.int32, (slot_count * device_count, mat_count), 0)
    ).astype(jnp.bfloat16)
    flat_rows = nesterov.reshape(mat_count, row_count * col_count)
    outgoing = jnp.dot(selector, flat_rows, preferred_element_type=jnp.float32).astype(jnp.bfloat16)
    outgoing = outgoing.reshape(slot_count, dp_count, owner_count, row_count, col_count)
    received = lax.all_to_all(
        lax.all_to_all(outgoing, "dp", split_axis=1, concat_axis=1, tiled=True),
        "owner",
        split_axis=2,
        concat_axis=2,
        tiled=True,
    )
    matrices = received.reshape(slot_count, device_count * row_count, col_count)
    finished = jnp.stack([orthogonalize(matrices[slot]) for slot in range(slot_count)])
    owned_update = (update_scale * finished.astype(jnp.float32)).astype(jnp.bfloat16)[:, None]
    returned = lax.all_to_all(
        lax.all_to_all(
            finished.reshape(slot_count, dp_count, owner_count, row_count, col_count),
            "dp",
            split_axis=1,
            concat_axis=1,
            tiled=True,
        ),
        "owner",
        split_axis=2,
        concat_axis=2,
        tiled=True,
    )
    returned = returned.reshape(slot_count * device_count, row_count * col_count)
    picked = lax.dot_general(
        selector, returned, (((0,), (0,)), ((), ())), preferred_element_type=jnp.float32
    )
    mine = picked.reshape(mat_count, row_count, col_count)
    update = update_scale * mine
    return (new_momentum, update, owned_update)


def solution(mesh):
    in_specs = (P(None, ("dp", "owner"), None), P(None, ("dp", "owner"), None), P())
    out_specs = (
        P(None, ("dp", "owner"), None),
        P(None, ("dp", "owner"), None),
        P(None, ("dp", "owner"), None, None),
    )
    return jax.shard_map(shards, mesh=mesh, in_specs=in_specs, out_specs=out_specs, check_vma=False)
```

profile of v0, /device:TPU:34, one launch (start us, length us, event | category | flops | bytes accessed | tf_op | source)
XLA Modules:
  0.0 323.3 jit_solution(287869679780489072)
XLA Ops:
  0.6 0.9 convert_reduce_fusion
  1.6 0.7 multiply_add_fusion
  2.3 4.6 %fusion.4 = (bf16[192,4,768]{2,1,0:T(4,128)(2,1)S(1)}, f32[192,4,768]{2,1,0:T(4,128)}) fusion(bf16[192,4,768]{2,1,0:T(4,128)(2,1)} %param.4, f32[192,4,768]{2,1,0:T(4,128)} %param.3), kind=kLoop, calls=%fused_computation.17 | loop fusion | flops 3538944 | bytes 7077888 | tf_op jit(solution)/shard_map/convert_element_type | solution.py:57
  6.9 0.2 copy.52
  7.1 1.1 convolution_convert_fusion
  8.2 1.7 copy.36
  9.9 44.3 %all_to_all.20 = bf16[2,32,8,4,768]{4,3,2,0,1:T(4,128)(2,1)S(1)} all-to-all(bf16[2,32,8,4,768]{4,3,2,0,1:T(4,128)(2,1)S(1)} %copy.36), channel_id=1, replica_groups=mesh['dp'=32,'owner'=8] {'dp'}, dimensions={1} | all-to-all | bytes 6291456 | tf_op jit(solution)/shard_map/all_to_all | solution.py:68
  54.2 1.7 copy.37
  56.0 81.6 %all_to_all.21 = bf16[2,32,8,4,768]{4,1,3,0,2:T(8,128)(2,1)S(1)} all-to-all(bf16[2,32,8,4,768]{4,1,3,0,2:T(8,128)(2,1)S(1)} %copy.37), channel_id=1, replica_groups=mesh['dp'=32,'owner'=8] {'owner'}, dimensions={2} | all-to-all | bytes 6291456 | tf_op jit(solution)/shard_map/all_to_all | solution.py:67
  137.6 1.4 fusion
  140.4 0.7 fusion.1
  141.1 2.5 bitcast_convert_fusion.1
  143.6 1.2 copy.39
  144.8 2.5 bitcast_convert_fusion
  147.3 1.2 copy.41
  148.5 1.3 convert_element_type.129
  149.8 5.4 %add_convert_fusion.3 = bf16[1024,768]{1,0:T(8,128)(2,1)S(1)} fusion(bf16[1024,768]{1,0:T(8,128)(2,1)} %convert_element_type.129, bf16[768,768]{1,0:T(8,128)(2,1)} %bitcast_convert_fusion.1), kind=kOutput, calls=%fused_computation.14 | convolution fusion | flops 2120024064 | bytes 4325376 | tf_op jit(solution)/shard_map/dot_general | solution.py:34
  155.2 0.0 copy-start.2
  155.2 1.1 copy-done.2
  156.4 2.5 convolution_convert_fusion.2
  158.8 5.4 %add_convert_fusion.2 = bf16[1024,768]{1,0:T(8,128)(2,1)S(1)} fusion(bf16[1024,768]{1,0:T(8,128)(2,1)} %copy-done.2, bf16[768,768]{1,0:T(8,128)(2,1)} %convolution_convert_fusion.2), kind=kOutput, calls=%fused_computation.13 | convolution fusion | flops 2120024064 | bytes 4325376 | tf_op jit(solution)/shard_map/dot_general | solution.py:34
  164.2 0.0 copy-start
  164.2 1.5 convert_element_type.142
  165.7 5.3 %add_convert_fusion.1 = bf16[1024,768]{1,0:T(8,128)(2,1)S(1)} fusion(bf16[1024,768]{1,0:T(8,128)(2,1)} %convert_element_type.142, bf16[768,768]{1,0:T(8,128)(2,1)} %bitcast_convert_fusion), kind=kOutput, calls=%fused_computation.12 | convolution fusion | flops 2120024064 | bytes 4325376 | tf_op jit(solution)/shard_map/dot_general | solution.py:34
  171.1 0.0 copy-start.3
  171.1 1.1 copy-done.3
  172.2 2.5 convolution_convert_fusion.1
  174.7 5.3 %add_convert_fusion = bf16[1024,768]{1,0:T(8,128)(2,1)S(1)} fusion(bf16[1024,768]{1,0:T(8,128)(2,1)} %copy-done.3, bf16[768,768]{1,0:T(8,128)(2,1)} %convolution_convert_fusion.1), kind=kOutput, calls=%fused_computation.11 | convolution fusion | flops 2120024064 | bytes 4325376 | tf_op jit(solution)/shard_map/dot_general | solution.py:34
  180.0 0.0 copy-start.1
  180.0 1.6 stack.16
  181.6 0.0 copy-done
  181.6 1.3 stack.15
  182.9 0.0 copy-done.1
  182.9 3.9 %pad_maximum_fusion = bf16[2,32,8,4,768]{4,3,2,0,1:T(4,128)(2,1)S(1)} fusion(bf16[1,32,8,4,768]{4,3,2,0,1:T(4,128)(2,1)} %bitcast.67, bf16[1,32,8,4,768]{4,3,2,0,1:T(4,128)(2,1)} %bitcast.68), kind=kLoop, calls=%fused_computation.10 | loop fusion | flops 1572864 | bytes 6291456 | tf_op jit(solution)/shard_map/stack | solution.py:75
  186.8 42.3 %all_to_all.22 = bf16[2,32,8,4,768]{4,3,2,0,1:T(4,128)(2,1)S(1)} all-to-all(bf16[2,32,8,4,768]{4,3,2,0,1:T(4,128)(2,1)S(1)} %pad_maximum_fusion), channel_id=1, replica_groups=mesh['dp'=32,'owner'=8] {'dp'}, dimensions={1} | all-to-all | bytes 6291456 | tf_op jit(solution)/shard_map/all_to_all | solution.py:78
  229.2 3.2 copy.44
  232.3 5.0 %all-to-all-start.3 = ((bf16[2,32,8,4,768]{4,3,1,0,2:T(4,128)(2,1)}), bf16[2,32,8,4,768]{4,3,1,0,2:T(4,128)(2,1)S(1)}, u32[]{:S(2)}, u32[]{:S(2)}) async-start(bf16[2,32,8,4,768]{4,3,1,0,2:T(4,128)(2,1)} %copy.44), calls=%async_computation.3 | async-start | bytes 6291456 | tf_op jit(solution)/shard_map/all_to_all | solution.py:77
  237.4 4.1 %multiply_convert_fusion = bf16[2,1,1024,768]{3,2,1,0:T(8,128)(2,1)} fusion(bf16[1,1,1024,768]{3,2,1,0:T(8,128)(2,1)} %bitcast.66, bf16[1,1,1024,768]{3,2,1,0:T(8,128)(2,1)} %bitcast.65), kind=kLoop, calls=%fused_computation | loop fusion | flops 6291456 | bytes 6291456 | tf_op jit(solution)/shard_map/convert_element_type | solution.py:76
  241.5 69.5 %all-to-all-done.3 = bf16[2,32,8,4,768]{4,3,1,0,2:T(4,128)(2,1)S(1)} async-done(((bf16[2,32,8,4,768]{4,3,1,0,2:T(4,128)(2,1)}), bf16[2,32,8,4,768]{4,3,1,0,2:T(4,128)(2,1)S(1)}, u32[]{:S(2)}, u32[]{:S(2)}) %all-to-all-start.3) | async-done | bytes 3145760 | tf_op jit(solution)/shard_map/all_to_all | solution.py:77
  311.0 5.0 %copy.53 = bf16[64,8,4,768]{3,1,2,0:T(8,128)(2,1)} copy(bf16[64,8,4,768]{3,2,0,1:T(4,128)(2,1)S(1)} %bitcast.62) | data formatting | bytes 6291456
  316.0 3.2 copy.46
  319.2 1.2 convolution_multiply_fusion
  320.4 2.9 copy.47
Async XLA Ops:
  155.2 1.1 copy-start.2
  164.2 17.4 %copy-start = (bf16[1024,768]{1,0:T(8,128)(2,1)}, bf16[1024,768]{1,0:T(8,128)(2,1)S(1)}, u32[]{:S(2)}) copy-start(bf16[1024,768]{1,0:T(8,128)(2,1)S(1)} %add_convert_fusion.2) | copy-start | bytes 4718596
  171.1 1.1 copy-start.3
  180.0 2.9 copy-start.1
  232.3 78.7 %all-to-all-start.3 = ((bf16[2,32,8,4,768]{4,3,1,0,2:T(4,128)(2,1)}), bf16[2,32,8,4,768]{4,3,1,0,2:T(4,128)(2,1)S(1)}, u32[]{:S(2)}, u32[]{:S(2)}) async-start(bf16[2,32,8,4,768]{4,3,1,0,2:T(4,128)(2,1)} %copy.44), calls=%async_computation.3 | async-start | bytes 6291456 | tf_op jit(solution)/shard_map/all_to_all | solution.py:77
where the time goes:
time: 326 us; the launch traced here: 323 us
  blocking collectives  168 us (52%)
  waiting for transfers between devices  69.5 us (21%)
  matrix products  33.6 us (10%)
  local copies, waits for them, and re-layouts  28.3 us (9%)
  other arithmetic  16.4 us (5%)
  starting transfers between devices  5.01 us (2%)
    all_to_all x1, blocking collectives, shards(): lax.all_to_all(lax.all_to_all(outgoing, 'dp', split_axis=1, concat_axis=1...  81.6 us
    all_to_all x1, waiting for transfers between devices, shards(): lax.all_to_all(lax.all_to_all(finished.reshape(slot_count, dp_count, owne...  69.5 us
    all_to_all x1, blocking collectives, shards(): lax.all_to_all(outgoing, 'dp', split_axis=1, concat_axis=1, tiled=True)  44.3 us
    all_to_all x1, blocking collectives, shards(): lax.all_to_all(finished.reshape(slot_count, dp_count, owner_count, row_co...  42.3 us
    dot_general x4, matrix products, orthogonalize(): jnp.dot(iterate, poly, preferred_element_type=jnp.float32)  21.5 us
    unnamed x11, local copies, waits for them, and re-layouts  10.4 us
    dot_general x4, matrix products, orthogonalize(): lax.dot_general(iterate, iterate, (((0,), (0,)), ((), ())), preferred_ele...  9.83 us
  transfers between devices with their start and end apart: 1, of which 1 were waited for; matrix products, arithmetic and copies ran while one was open for 1% of the time, Pallas kernels for 0%

commit v1 on v0

v1 whole, which is shorter than its diff:
```python
import functools
import math

import jax
import jax.numpy as jnp
from jax import lax
from jax.experimental import pallas as pl
from jax.experimental.pallas import tpu as pltpu
from jax.sharding import PartitionSpec as P

ITERS = 2
CAP = 2

momentum_decay = 0.95
quintic_one = 3.4445
quintic_two = -4.775
quintic_three = 2.0315
norm_epsilon = 1e-07

HOSTS, WAYS, WORK, OWNED, LEFT = 0, 16, 32, 40, 48
PLANES, COLUMNS, TABLE_ROWS = 8, 128, 56
HOST, MATRIX, LIST_ROWS = 0, 1, 8
FAR, ROUNDS = 63, 20


def chip_steps():
    steps = ([], [], [])
    for x in range(4):
        for y in range(4):
            for core, way in ((0, 1), (1, -1)):
                here = (x * 4 + y) * 2 + core
                steps[0].append((here, here + way))
                steps[1].append((here, ((x + way) % 4 * 4 + y) * 2 + core))
                steps[2].append((here, (x * 4 + (y + way) % 4) * 2 + core))
    return steps


def neighbours():
    lane = lax.broadcasted_iota(jnp.int32, (PLANES, COLUMNS), 1)
    core, y = lane & 1, (lane >> 1) & 3

    def at(values, way):
        return pltpu.roll(values, (COLUMNS - way) % COLUMNS, 1)

    def flip(values):
        return jnp.where(core == 0, at(values, 1), at(values, -1))

    def along_x(values, sign):
        return jnp.where(core == 0, at(values, 8 * sign), at(values, -8 * sign))

    def along_y(values, sign):
        up = jnp.where(y == 3, at(values, -6), at(values, 2))
        down = jnp.where(y == 0, at(values, 6), at(values, -2))
        return jnp.where((core == 0) == (sign > 0), up, down)

    pull = (flip, lambda values: along_x(values, -1), lambda values: along_y(values, -1))
    push = (flip, lambda values: along_x(values, 1), lambda values: along_y(values, 1))
    return pull, push


def search_turn(work, label, waiting):
    pull, push = neighbours()
    best, choice = jnp.full_like(work, FAR), jnp.zeros_like(work)
    for k in range(3):
        there = pull[k](label * 8 + work + 1)
        value = jnp.where((there & 7) == k + 2, FAR, there >> 3)
        choice = jnp.where(value < best, k + 1, choice)
        best = jnp.minimum(value, best)
    message = best * 8 + jnp.where(waiting > 0, choice, 0)
    moved = jnp.where(work == 0, best + 1, 0)
    taken = jnp.zeros_like(work)
    for k in range(3):
        there = push[k](message)
        moved = jnp.where(work == k + 1, (there >> 3) + 1, moved)
        taken = jnp.where((taken == 0) & ((there & 7) == k + 1), k + 1, taken)
    label = jnp.minimum(jnp.maximum(label, moved), FAR)
    waiting = waiting + jnp.where((taken > 0) & (work == 0), 1, 0)
    for k in range(3):
        waiting = waiting + pull[k](jnp.where((taken > 0) & (work == k + 1), 1, 0) - jnp.where(taken == k + 1, 1, 0))
    return jnp.where(taken > 0, taken, work), label, waiting


def search_rest(work, label, waiting):
    def going(state):
        count, _, _, _, left = state
        return (count < ROUNDS) & (left > 0)

    def turn(state):
        count, *found, _ = state
        found = search_turn(*search_turn(*found))
        return count + 2, *found, jnp.sum(found[2])

    _, work, _, _, left = lax.while_loop(going, turn, (jnp.int32(0), work, label, waiting, jnp.sum(waiting)))
    return work, left


def iota(rows, cols, axis):
    return lax.broadcasted_iota(jnp.int32, (rows, cols), axis)


def column(row):
    n = row.shape[1]
    return jnp.sum(jnp.where(iota(n, n, 0) == iota(n, n, 1), row, 0.0), axis=1, keepdims=True)


def count_owned(planes, owner_col):
    mats = owner_col.shape[0]
    owned = jnp.zeros((PLANES, COLUMNS), jnp.float32)
    index = (iota(mats, COLUMNS, 1) & 31) * planes
    for p in range(planes):
        hits = jnp.sum(jnp.where(owner_col == index + p, 1.0, 0.0), axis=0, keepdims=True)
        owned = jnp.where(iota(PLANES, COLUMNS, 0) == p, hits, owned)
    return owned.astype(jnp.int32)


def rank_of(owner_row, owner_col):
    mats = owner_col.shape[0]
    earlier = (owner_col == owner_row) & (iota(mats, mats, 1) < iota(mats, mats, 0))
    return jnp.sum(jnp.where(earlier, 1.0, 0.0), axis=1, keepdims=True).astype(jnp.int32)


def fill_lists(planes, owner_col, rank_col, table_ref, lists_ref):
    mats, devices = owner_col.shape[0], lists_ref.shape[1]
    shift = planes.bit_length() - 1
    at_dp = jnp.where(iota(mats, COLUMNS, 1) == owner_col >> shift, 1.0, 0.0)
    hosts = table_ref[HOSTS : HOSTS + CAP * PLANES, :].astype(jnp.float32)
    found = lax.dot_general(at_dp, hosts, (((1,), (1,)), ((), ())), preferred_element_type=jnp.float32)
    wanted = iota(mats, CAP * PLANES, 1) == rank_col * PLANES + (owner_col & (planes - 1))
    host_col = jnp.sum(jnp.where(wanted, found, 0.0), axis=1, keepdims=True)
    host_row = jnp.sum(jnp.where(iota(mats, mats, 0) == iota(mats, mats, 1), host_col, 0.0), axis=0, keepdims=True)
    here = host_col.astype(jnp.int32) == iota(mats, devices, 1)
    number = (iota(mats, devices, 0) + 1).astype(jnp.float32)
    matrix_row = jnp.sum(jnp.where(here, number, 0.0), axis=0, keepdims=True) - 1.0
    lists_ref[...] = jnp.zeros_like(lists_ref)
    lists_ref[HOST : HOST + 1, :mats] = host_row.astype(jnp.int32)
    lists_ref[MATRIX : MATRIX + 1, :] = matrix_row.astype(jnp.int32)


def fill_table(planes, owned, work, left, table_ref):
    plane, lane = (iota(PLANES, COLUMNS, axis) for axis in (0, 1))
    pull, _ = neighbours()
    device = (lane & 31) * planes + plane
    none = jnp.full_like(owned, -1)
    hosts, ways = [none, none], [none, none]
    options = [(work == 0, device, 0)] + [(pull[k](work) == k + 1, pull[k](device), k + 1) for k in range(3)]
    for chosen, host, way in options:
        for slot in (1, 0):
            free = hosts[slot] < 0 if slot == 0 else (hosts[1] < 0) & (hosts[0] >= 0)
            hosts[slot] = jnp.where(chosen & free, host, hosts[slot])
            ways[slot] = jnp.where(chosen & free, way, ways[slot])
    for slot in range(CAP):
        table_ref[HOSTS + slot * PLANES : HOSTS + (slot + 1) * PLANES, :] = hosts[slot]
        table_ref[WAYS + slot * PLANES : WAYS + (slot + 1) * PLANES, :] = ways[slot]
    table_ref[WORK : WORK + PLANES, :] = work
    table_ref[OWNED : OWNED + PLANES, :] = owned
    table_ref[LEFT : LEFT + PLANES, :] = jnp.zeros_like(owned) + left


def place_left(planes, devices, table_ref):
    shift = planes.bit_length() - 1

    def each(i, idle):
        device = i // CAP
        plane, dp = device & (planes - 1), device >> shift
        host_row = HOSTS + (i % CAP) * PLANES + plane
        alone = (table_ref[OWNED + plane, dp] > i % CAP) & (table_ref[host_row, dp] < 0)

        def find(at):
            return lax.while_loop(lambda at: table_ref[WORK + (at & (planes - 1)), at >> shift] >= 0, lambda at: at + 1, at)

        @pl.when(alone)
        def _():
            table_ref[host_row, dp] = find(idle)

        return lax.cond(alone, lambda: find(idle) + 1, lambda: idle)

    lax.fori_loop(0, CAP * devices, each, jnp.int32(0))


def start_kernel(
    planes, owner_ref, momentum_ref, grad_ref, table_ref, lists_ref, new_ref, out_ref,
    new, grad, fixed, hosts, in_sem, out_sem, table_sem, rows_sem
):
    chunks = in_sem.shape[1]
    block = new.shape[0] // chunks

    def part(chunk):
        return pl.ds(chunk * block, block)

    def copies_in(chunk):
        return (
            pltpu.make_async_copy(momentum_ref.at[part(chunk)], new.at[part(chunk)], in_sem.at[0, chunk]),
            pltpu.make_async_copy(grad_ref.at[part(chunk)], grad.at[part(chunk)], in_sem.at[1, chunk]),
        )

    def copy_out(chunk):
        return pltpu.make_async_copy(new.at[part(chunk)], new_ref.at[part(chunk)], out_sem.at[chunk])

    for chunk in range(chunks):
        for copy in copies_in(chunk):
            copy.start()
    owner_row = owner_ref[...]
    owner_col = column(owner_row.astype(jnp.float32)).astype(jnp.int32)
    owned = count_owned(planes, owner_col)
    rank_col = rank_of(owner_row, owner_col)

    def each_chunk(chunk, found):
        for copy in copies_in(chunk):
            copy.wait()
        for i in range(block):
            mat = chunk * block + i
            value = grad[mat].astype(jnp.float32)
            result = momentum_decay * new[mat] + value
            new[mat] = result
            grad[mat] = (value + momentum_decay * result).astype(grad.dtype)
        copy_out(chunk).start()
        return search_turn(*found)

    found = (jnp.where(owned > 0, 0, -1), jnp.where(owned > 0, 1, 0), jnp.maximum(owned - 1, 0))
    work, left = search_rest(*lax.fori_loop(0, chunks, each_chunk, found))
    fill_table(planes, owned, work, left, table_ref)

    @pl.when(left > 0)
    def _():
        copy = pltpu.make_async_copy(table_ref, fixed, table_sem)
        copy.start()
        copy.wait()
        place_left(planes, out_ref.shape[0], fixed)
        copy = pltpu.make_async_copy(fixed, table_ref, table_sem)
        copy.start()
        copy.wait()

    fill_lists(planes, owner_col, rank_col, table_ref, lists_ref)
    copy = pltpu.make_async_copy(lists_ref, hosts, table_sem)
    copy.start()
    copy.wait()

    def each(mat, _):
        pltpu.make_async_copy(grad.at[mat], out_ref.at[hosts[HOST, mat]], rows_sem).start()

    mats = new.shape[0]
    lax.fori_loop(0, mats, each, None, unroll=8 if mats % 8 == 0 else 1)
    pltpu.make_async_copy(grad, out_ref.at[pl.ds(0, mats)], rows_sem).wait()
    for chunk in range(chunks):
        copy_out(chunk).wait()


def start(owner_table, momentum, grad, planes, devices, chunks=6):
    mats, rows, cols = momentum.shape
    while mats % chunks:
        chunks -= 1
    hbm = pl.BlockSpec(memory_space=pltpu.HBM)
    outgoing = (devices, rows, cols)
    return pl.pallas_call(
        functools.partial(start_kernel, planes),
        grid=(1,),
        in_specs=[pl.BlockSpec((1, mats), lambda *_: (0, 0)), hbm, hbm],
        out_specs=[
            pl.BlockSpec((TABLE_ROWS, COLUMNS), lambda *_: (0, 0)),
            pl.BlockSpec((LIST_ROWS, devices), lambda *_: (0, 0)),
            hbm,
            hbm,
        ],
        scratch_shapes=[
            pltpu.VMEM(momentum.shape, momentum.dtype),
            pltpu.VMEM(grad.shape, grad.dtype),
            pltpu.SMEM((TABLE_ROWS, COLUMNS), jnp.int32),
            pltpu.SMEM((LIST_ROWS, devices), jnp.int32),
            pltpu.SemaphoreType.DMA((2, chunks)),
            pltpu.SemaphoreType.DMA((chunks,)),
            pltpu.SemaphoreType.DMA,
            pltpu.SemaphoreType.DMA,
        ],
        out_shape=[
            jax.ShapeDtypeStruct((TABLE_ROWS, COLUMNS), jnp.int32),
            jax.ShapeDtypeStruct((LIST_ROWS, devices), jnp.int32),
            jax.ShapeDtypeStruct(momentum.shape, jnp.float32),
            jax.ShapeDtypeStruct(outgoing, jnp.bfloat16),
        ],
        compiler_params=pltpu.CompilerParams(vmem_limit_bytes=60 * 1024 * 1024),
        name="start",
    )(owner_table.reshape(1, mats), momentum, grad)


def orthogonalize_kernel(scale, x_ref, out_ref, iterate_ref, gram_ref, poly_ref):
    rows, cols = x_ref.shape
    tile, side = min(256, rows), min(256, cols) if cols % 256 == 0 else 128
    f32, bf16 = jnp.float32, jnp.bfloat16
    starts = range(0, cols, side)

    def put(ref, i, block):
        ref[i : i + side, i:] = block
        for j in range(i + side, cols, side):
            ref[j : j + side, i : i + side] = block[:, j - i : j - i + side].T

    def gram_rows(ref, i):
        return lax.dot_general(ref[:, i : i + side], ref[:, i:], (((0,), (0,)), ((), ())), preferred_element_type=f32)

    def poly():
        for i in starts:
            square = jnp.dot(gram_ref[i : i + side, :], gram_ref[:, i:], preferred_element_type=f32)
            put(poly_ref, i, (quintic_two * gram_ref[i : i + side, i:].astype(f32) + quintic_three * square).astype(bf16))

    def apply(source_ref, target_ref, factor, last):
        for i in range(0, rows, tile):
            part = source_ref[i : i + tile, :]
            step = quintic_one * part.astype(f32) + jnp.dot(part, poly_ref[...], preferred_element_type=f32)
            step = (step * factor).astype(bf16) if factor is not None else step.astype(bf16)
            step = step * jnp.asarray(scale, bf16) if last else step
            target_ref[i : i + tile, :] = step

    gram = [gram_rows(x_ref, i) for i in starts]
    diagonal = lax.broadcasted_iota(jnp.int32, (side, side), 0) == lax.broadcasted_iota(jnp.int32, (side, side), 1)
    squares = sum(jnp.where(diagonal, block[:, :side], 0.0) for block in gram)
    trace = jnp.sum(jnp.sum(squares, axis=0, keepdims=True), axis=1, keepdims=True)
    factor = 1.0 / (jnp.sqrt(trace) + norm_epsilon)
    for i, block in zip(starts, gram):
        put(gram_ref, i, (block * factor * factor).astype(bf16))
    poly()
    apply(x_ref, iterate_ref, factor, False)
    for step in range(1, ITERS):
        for i in starts:
            put(gram_ref, i, gram_rows(iterate_ref, i).astype(bf16))
        poly()
        apply(iterate_ref, out_ref, None, True)


def orthogonalize(matrix, scale):
    rows, cols = matrix.shape
    return pl.pallas_call(
        functools.partial(orthogonalize_kernel, scale),
        out_shape=jax.ShapeDtypeStruct((rows, cols), jnp.bfloat16),
        scratch_shapes=[
            pltpu.VMEM((rows, cols), jnp.bfloat16),
            pltpu.VMEM((cols, cols), jnp.bfloat16),
            pltpu.VMEM((cols, cols), jnp.bfloat16),
        ],
        compiler_params=pltpu.CompilerParams(vmem_limit_bytes=24 * 1024 * 1024),
        cost_estimate=pl.CostEstimate(flops=ITERS * 2 * cols * cols * (2 * rows + cols), bytes_accessed=4 * rows * cols, transcendentals=0),
        name="orthogonalize",
    )(matrix)


def begin_kernel(table_ref, *refs):
    sources, (owned_ref, held_ref, sem) = refs[:-3], refs[-3:]
    plane, dp = lax.axis_index("owner"), lax.axis_index("dp")
    ways = [table_ref[WAYS + slot * PLANES + plane, dp] for slot in range(CAP)]

    def bring(act):
        for slot, way in enumerate(ways):
            for k, source in enumerate(sources):

                @pl.when(way == k)
                def _():
                    act(pltpu.make_async_copy(source, held_ref.at[slot], sem.at[slot]))

    bring(lambda copy: copy.start())
    for slot, way in enumerate(ways):

        @pl.when(way < 0)
        def _():
            held_ref[slot] = jnp.zeros_like(held_ref[slot])

    bring(lambda copy: copy.wait())
    copy = pltpu.make_async_copy(held_ref, owned_ref, sem.at[CAP])
    copy.start()
    copy.wait()


def begin(table, sources):
    hbm = pl.BlockSpec(memory_space=pltpu.HBM)
    shape = (CAP, *sources[0].shape)
    return pl.pallas_call(
        begin_kernel,
        grid_spec=pltpu.PrefetchScalarGridSpec(
            num_scalar_prefetch=1,
            grid=(1,),
            in_specs=[hbm] * len(sources),
            out_specs=hbm,
            scratch_shapes=[pltpu.VMEM(shape, jnp.bfloat16), pltpu.SemaphoreType.DMA((CAP + 1,))],
        ),
        out_shape=jax.ShapeDtypeStruct(shape, jnp.bfloat16),
        compiler_params=pltpu.CompilerParams(vmem_limit_bytes=8 * 1024 * 1024),
        cost_estimate=pl.CostEstimate(flops=0, bytes_accessed=4 * math.prod(shape), transcendentals=0),
        name="begin",
    )(table, *sources)


def finish_kernel(lists_ref, rows_ref, _, update_ref, owned_ref, staged_ref, sem):
    devices = rows_ref.shape[0]
    count = min(32, devices)

    def each(chunk, _):
        first = chunk * count
        staged_ref[pl.ds(first, count)] = rows_ref[pl.ds(first, count)].astype(jnp.float32)
        for i in range(count):
            matrix = lists_ref[MATRIX, first + i]

            @pl.when(matrix >= 0)
            def _():
                pltpu.make_async_copy(staged_ref.at[first + i], update_ref.at[matrix], sem).start()

    lax.fori_loop(0, devices // count, each, None)
    pltpu.make_async_copy(staged_ref.at[pl.ds(0, update_ref.shape[0])], update_ref, sem).wait()


def finish(lists, arrived, owned, mats):
    hbm = pl.BlockSpec(memory_space=pltpu.HBM)
    _, rows, cols = arrived.shape
    return pl.pallas_call(
        finish_kernel,
        grid_spec=pltpu.PrefetchScalarGridSpec(
            num_scalar_prefetch=1,
            grid=(1,),
            in_specs=[pl.BlockSpec(arrived.shape, lambda *_: (0, 0, 0)), hbm],
            out_specs=[hbm, hbm],
            scratch_shapes=[pltpu.VMEM(arrived.shape, jnp.float32), pltpu.SemaphoreType.DMA],
        ),
        out_shape=[
            jax.ShapeDtypeStruct((mats, rows, cols), jnp.float32),
            jax.ShapeDtypeStruct(owned.shape, owned.dtype),
        ],
        input_output_aliases={2: 1},
        compiler_params=pltpu.CompilerParams(vmem_limit_bytes=20 * 1024 * 1024),
        name="finish",
    )(lists, arrived, owned)


def left_kernel(planes, slot, table_ref, arrived_ref, out_ref):
    shift = planes.bit_length() - 1

    def each(i, _):
        host = table_ref[HOSTS + slot * PLANES + (i & (planes - 1)), i >> shift]
        out_ref[i] = arrived_ref[jnp.maximum(host, 0)]

    lax.fori_loop(0, out_ref.shape[0], each, None)


def left_rows(table, arrived, planes, slot):
    whole = pl.BlockSpec(arrived.shape, lambda *_: (0, 0, 0))
    return pl.pallas_call(
        functools.partial(left_kernel, planes, slot),
        grid_spec=pltpu.PrefetchScalarGridSpec(num_scalar_prefetch=1, grid=(1,), in_specs=[whole], out_specs=whole),
        out_shape=jax.ShapeDtypeStruct(arrived.shape, arrived.dtype),
        compiler_params=pltpu.CompilerParams(vmem_limit_bytes=14 * 1024 * 1024),
        name="left",
    )(table, arrived)


def shards(momentum, grad, owner_table):
    dp_count = lax.axis_size("dp")
    planes = lax.axis_size("owner")
    devices = dp_count * planes
    mats, rows, cols = momentum.shape
    whole_rows = devices * rows
    both = ("dp", "owner")
    with jax.named_scope("start"):
        table, lists, new_momentum, outgoing = start(owner_table, momentum, grad, planes, devices)
    with jax.named_scope("gather_matrix"):
        received = lax.all_to_all(outgoing, both, 0, 0, tiled=True)
        matrix = received.reshape(whole_rows, cols)
    with jax.named_scope("orthogonalize"):
        mine = orthogonalize(matrix, math.sqrt(whole_rows))
    with jax.named_scope("return_rows"):
        arrived = lax.all_to_all(mine.reshape(devices, rows, cols), both, 0, 0, tiled=True)
    with jax.named_scope("owned"):
        owned = begin(table, [mine, *(lax.ppermute(mine, "dp", step) for step in chip_steps())])

    def with_left(owned, arrived):
        plane, dp = lax.axis_index("owner"), lax.axis_index("dp")
        slots = []
        for slot in range(CAP):
            matrix = lax.all_to_all(left_rows(table, arrived, planes, slot), both, 0, 0, tiled=True)
            slots.append(jnp.where(table[OWNED + plane, dp] > slot, matrix.reshape(whole_rows, cols), 0))
        return jnp.stack(slots)

    with jax.named_scope("left"):
        owned = lax.cond(table[LEFT, 0] > 0, with_left, lambda owned, arrived: owned, owned, arrived)
    with jax.named_scope("finish"):
        update, owned = finish(lists, arrived, owned, mats)
    return new_momentum, update, owned[:, None]


def solution(mesh):
    in_specs = (P(None, ("dp", "owner"), None), P(None, ("dp", "owner"), None), P())
    out_specs = (
        P(None, ("dp", "owner"), None),
        P(None, ("dp", "owner"), None),
        P(None, ("dp", "owner"), None, None),
    )
    return jax.shard_map(shards, mesh=mesh, in_specs=in_specs, out_specs=out_specs, check_vma=False)
```

time: 326 us -> 127 us (0.39)
  blocking collectives: 168 us -> 56.5 us
  waiting for transfers between devices: 69.5 us -> 34.9 us
  matrix products: 33.6 us -> 0 us
  local copies, waits for them, and re-layouts: 28.3 us -> 2.92 us
  Pallas kernels: 0 us -> 19.5 us
  other arithmetic: 16.4 us -> 0 us
  starting transfers between devices: 5.01 us -> 10.3 us
    all_to_all x3 -> x1, blocking collectives: 168 us -> 56.5 us  [shards(): received = lax.all_to_all(outgoing, both, 0, 0, tiled=True)]
    all_to_all x1, waiting for transfers between devices: 69.5 us -> 4.26 us  [shards(): lax.all_to_all(mine.reshape(devices, rows, cols), both, 0, 0, tiled=True)]
    dot_general x10 -> x0, matrix products: 33.6 us -> none  [the longest x4 21.5 us: orthogonalize(): jnp.dot(iterate, poly, preferred_element_type=jnp.float32)]
    ppermute x0 -> x3, waiting for transfers between devices: none -> 30.6 us  [shards(): lax.ppermute(mine, 'dp', step)]
    pallas_call x0 -> x4, Pallas kernels: none -> 19.5 us  [the longest x1 8.15 us: start(): pl.pallas_call(functools.partial(start_kernel, planes), grid=(1,), in_spe...]
    unnamed x11 -> x2, local copies, waits for them, and re-layouts: 10.4 us -> 0.7 us
    convert_element_type x3 -> x0, other arithmetic: 9.47 us -> none  [the longest x1 4.65 us: shards(): (grad_values + momentum_decay * new_momentum).astype(jnp.bfloat16)]
    convert_element_type x4 -> x0, local copies, waits for them, and re-layouts: 5.3 us -> none  [orthogonalize(): iterate = (values / (frobenius + norm_epsilon)).astype(jnp.bfloat16)]
  transfers between devices with their start and end apart: 1 -> 4, of which waited for: 1 -> 2; matrix products, arithmetic and copies ran while one was open for 1% -> 0% of each run, Pallas kernels for 0% -> 2%
where the time goes in v1:
time: 127 us; the launch traced here: 126 us
  blocking collectives  56.5 us (44%)
  waiting for transfers between devices  34.9 us (27%)
  Pallas kernels  19.5 us (15%)
  starting transfers between devices  10.3 us (8%)
  local copies, waits for them, and re-layouts  2.92 us (2%)
  between operations  1.51 us (1%)
    all_to_all x1, blocking collectives, shards(): received = lax.all_to_all(outgoing, both, 0, 0, tiled=True)  56.5 us
    ppermute x3, waiting for transfers between devices, shards(): lax.ppermute(mine, 'dp', step)  30.6 us
    pallas_call x1, Pallas kernels, start(): pl.pallas_call(functools.partial(start_kernel, planes), grid=(1,), in_spe...  8.15 us
    all_to_all x1, starting transfers between devices, shards(): lax.all_to_all(mine.reshape(devices, rows, cols), both, 0, 0, tiled=True)  7.17 us
    pallas_call x1, Pallas kernels, orthogonalize(): pl.pallas_call(functools.partial(orthogonalize_kernel, scale), out_shape=...  6.02 us
    all_to_all x1, waiting for transfers between devices, shards(): lax.all_to_all(mine.reshape(devices, rows, cols), both, 0, 0, tiled=True)  4.26 us
    ppermute x3, starting transfers between devices, shards(): lax.ppermute(mine, 'dp', step)  3.09 us
    pallas_call x1, Pallas kernels, begin(): pl.pallas_call(begin_kernel, grid_spec=pltpu.PrefetchScalarGridSpec(num_s...  2.96 us
  transfers between devices with their start and end apart: 4, of which 2 were waited for; matrix products, arithmetic and copies ran while one was open for 0% of the time, Pallas kernels for 2%

profile of v1, /device:TPU:34, one launch (start us, length us, event | category | flops | bytes accessed | tf_op | source)
XLA Modules:
  0.0 125.6 jit_solution(14556806735141016891)
XLA Ops:
  0.6 8.2 %start.1 = (s32[56,128]{1,0:T(8,128)S(1)}, s32[8,256]{1,0:T(8,128)}, f32[192,4,768]{2,1,0:T(4,128)}, bf16[256,4,768]{2,1,0:T(4,128)(2,1)}) custom-call(s32[1,192]{1,0:T(1,128)} %bitcast.8, f32[192,4,768]{2,1,0:T(4,128)} %momentum_ref.1, bf16[192,4,768]{2,1,0:T(4,128)(2,1)} %grad_ref.1), custom_call_target="tpu_custom_call" | custom-call | tf_op jit(solution)/shard_map/start/start/pallas_call | solution.py:254
  8.8 56.5 %all_to_all.18 = bf16[256,4,768]{2,1,0:T(4,128)(2,1)S(1)} all-to-all(bf16[256,4,768]{2,1,0:T(4,128)(2,1)} %get-tuple-element.21), channel_id=1, replica_groups=mesh['dp'=32,'owner'=8] {'dp','owner'}, dimensions={0} | all-to-all | bytes 3145728 | tf_op jit(solution)/shard_map/gather_matrix/all_to_all | solution.py:460
  65.3 0.4 reshape.52.x_ref
  65.7 6.0 %orthogonalize.1.refs_0_ = bf16[1024,768]{1,0:T(8,128)(2,1)S(1)} custom-call(bf16[1024,768]{1,0:T(8,128)(2,1)S(1)} %reshape.52.x_ref), custom_call_target="tpu_custom_call" | custom-call | flops 6643777536 | bytes 3145728 | tf_op jit(solution)/shard_map/orthogonalize/orthogonalize/pallas_call | solution.py:330
  71.7 1.3 %reshape.53 = bf16[256,4,768]{2,1,0:T(4,128)(2,1)} reshape(bf16[1024,768]{1,0:T(8,128)(2,1)S(1)} %orthogonalize.1.refs_0_) | data formatting | bytes 3145728 | tf_op jit(solution)/shard_map/return_rows/reshape | solution.py:465
  73.0 7.2 %all-to-all-start.3 = ((bf16[256,4,768]{2,1,0:T(4,128)(2,1)}), bf16[256,4,768]{2,1,0:T(4,128)(2,1)S(1)}, u32[]{:S(2)}, u32[]{:S(2)}) async-start(bf16[256,4,768]{2,1,0:T(4,128)(2,1)} %reshape.53), calls=%async_computation.3 | async-start | bytes 3145728 | tf_op jit(solution)/shard_map/return_rows/all_to_all | solution.py:465
  80.2 1.6 %collective-permute-start.2 = (bf16[1024,768]{1,0:T(8,128)(2,1)S(1)}, bf16[1024,768]{1,0:T(8,128)(2,1)S(1)}, u32[]{:S(2)}, u32[]{:S(2)}) collective-permute-start(bf16[1024,768]{1,0:T(8,128)(2,1)S(1)} %orthogonalize.1.refs_0_), channel_id=1, source_target_pairs={{0,16},{8,56},{16,32},{24,8},{32,48},{40,24},{48,0},{56,40},{64,80... | collective-permute-start | bytes 4718600 | tf_op jit(solution)/shard_map/owned/ppermute | solution.py:467
  81.8 1.5 %collective-permute-start.1 = (bf16[1024,768]{1,0:T(8,128)(2,1)S(1)}, bf16[1024,768]{1,0:T(8,128)(2,1)S(1)}, u32[]{:S(2)}, u32[]{:S(2)}) collective-permute-start(bf16[1024,768]{1,0:T(8,128)(2,1)S(1)} %orthogonalize.1.refs_0_), channel_id=1, source_target_pairs={{0,64},{8,200},{16,80},{24,216},{32,96},{40,232},{48,112},{56,248}... | collective-permute-start | bytes 4718600 | tf_op jit(solution)/shard_map/owned/ppermute | solution.py:467
  83.3 0.0 collective-permute-start
  83.3 0.5 slice.3
  84.5 30.6 %collective-permute-done.2.refs_3_ = bf16[1024,768]{1,0:T(8,128)(2,1)S(1)} collective-permute-done((bf16[1024,768]{1,0:T(8,128)(2,1)S(1)}, bf16[1024,768]{1,0:T(8,128)(2,1)S(1)}, u32[]{:S(2)}, u32[]{:S(2)}) %collective-permute-start.2) | collective-permute-done | bytes 1572896 | tf_op jit(solution)/shard_map/owned/ppermute | solution.py:467
  115.1 0.0 collective-permute-done.1.refs_2_
  115.1 0.0 collective-permute-done.refs_1_
  115.1 3.0 %begin.1 = bf16[2,1024,768]{2,1,0:T(8,128)(2,1)} custom-call(s32[56,128]{1,0:T(8,128)S(1)} %get-tuple-element.22.table_ref, bf16[1024,768]{1,0:T(8,128)(2,1)S(1)} %orthogonalize.1.refs_0_, bf16[1024,768]{1,0:T(8,128)(2,1)S(1)} %collective-permute-done.refs_1_, bf16[1024,768]{1,0:T(8,128)(2,1)S(1)} %collective-permute-done.1.refs_2_, ...), custom_call_target="tpu_custom_call" | custom-call | bytes 6291456 | tf_op jit(solution)/shard_map/owned/begin/pallas_call | solution.py:373
  118.1 4.3 %all-to-all-done.3.rows_ref = bf16[256,4,768]{2,1,0:T(4,128)(2,1)S(1)} async-done(((bf16[256,4,768]{2,1,0:T(4,128)(2,1)}), bf16[256,4,768]{2,1,0:T(4,128)(2,1)S(1)}, u32[]{:S(2)}, u32[]{:S(2)}) %all-to-all-start.3) | async-done | bytes 1572896 | tf_op jit(solution)/shard_map/return_rows/all_to_all | solution.py:465
  122.3 0.0 copy-start
  122.3 0.7 copy-done
  123.0 2.3 %finish.1 = (f32[192,4,768]{2,1,0:T(4,128)}, bf16[2,1024,768]{2,1,0:T(8,128)(2,1)}) custom-call(s32[8,256]{1,0:T(8,128)S(1)} %copy-done, bf16[256,4,768]{2,1,0:T(4,128)(2,1)S(1)} %all-to-all-done.3.rows_ref, bf16[2,1024,768]{2,1,0:T(8,128)(2,1)} %get-tuple-element.28._), custom_call_target="tpu_custom_call", output_to_operand_aliasing={{1}: (2, {})} | custom-call | tf_op jit(solution)/shard_map/finish/finish/pallas_call | solution.py:410
  (1 shorter events, 0.0 us)
Async XLA Ops:
  73.0 49.3 %all-to-all-start.3 = ((bf16[256,4,768]{2,1,0:T(4,128)(2,1)}), bf16[256,4,768]{2,1,0:T(4,128)(2,1)S(1)}, u32[]{:S(2)}, u32[]{:S(2)}) async-start(bf16[256,4,768]{2,1,0:T(4,128)(2,1)} %reshape.53), calls=%async_computation.3 | async-start | bytes 3145728 | tf_op jit(solution)/shard_map/return_rows/all_to_all | solution.py:465
  80.2 34.9 %collective-permute-start.2 = (bf16[1024,768]{1,0:T(8,128)(2,1)S(1)}, bf16[1024,768]{1,0:T(8,128)(2,1)S(1)}, u32[]{:S(2)}, u32[]{:S(2)}) collective-permute-start(bf16[1024,768]{1,0:T(8,128)(2,1)S(1)} %orthogonalize.1.refs_0_), channel_id=1, source_target_pairs={{0,16},{8,56},{16,32},{24,8},{32,48},{40,24},{48,0},{56,40},{64,80... | collective-permute-start | bytes 4718600 | tf_op jit(solution)/shard_map/owned/ppermute | solution.py:467
  81.8 33.3 %collective-permute-start.1 = (bf16[1024,768]{1,0:T(8,128)(2,1)S(1)}, bf16[1024,768]{1,0:T(8,128)(2,1)S(1)}, u32[]{:S(2)}, u32[]{:S(2)}) collective-permute-start(bf16[1024,768]{1,0:T(8,128)(2,1)S(1)} %orthogonalize.1.refs_0_), channel_id=1, source_target_pairs={{0,64},{8,200},{16,80},{24,216},{32,96},{40,232},{48,112},{56,248}... | collective-permute-start | bytes 4718600 | tf_op jit(solution)/shard_map/owned/ppermute | solution.py:467
  83.3 31.8 %collective-permute-start = (bf16[1024,768]{1,0:T(8,128)(2,1)S(1)}, bf16[1024,768]{1,0:T(8,128)(2,1)S(1)}, u32[]{:S(2)}, u32[]{:S(2)}) collective-permute-start(bf16[1024,768]{1,0:T(8,128)(2,1)S(1)} %orthogonalize.1.refs_0_), channel_id=1, source_target_pairs={{0,8},{8,0},{16,24},{24,16},{32,40},{40,32},{48,56},{56,48},{64,72... | collective-permute-start | bytes 4718600 | tf_op jit(solution)/shard_map/owned/ppermute | solution.py:467
  122.3 0.7 copy-start

commit v2 on v1

--- a/solution.py
+++ b/solution.py
@@ -341,49 +341,118 @@
     )(matrix)
 
 
-def begin_kernel(table_ref, *refs):
-    sources, (owned_ref, held_ref, sem) = refs[:-3], refs[-3:]
+def begin_kernel(table_ref, lists_ref, mine_ref, owned_ref, again_ref, held_ref, zero_ref, in_sem, out_sem):
+    again_ref[...] = lists_ref[...]
     plane, dp = lax.axis_index("owner"), lax.axis_index("dp")
     ways = [table_ref[WAYS + slot * PLANES + plane, dp] for slot in range(CAP)]
-
-    def bring(act):
+    bring = pltpu.make_async_copy(mine_ref, held_ref, in_sem)
+    bring.start()
+    zero_ref[...] = jnp.zeros_like(zero_ref)
+    tile = zero_ref.shape[0]
+
+    def zeros(act):
         for slot, way in enumerate(ways):
-            for k, source in enumerate(sources):
-
-                @pl.when(way == k)
-                def _():
-                    act(pltpu.make_async_copy(source, held_ref.at[slot], sem.at[slot]))
-
-    bring(lambda copy: copy.start())
-    for slot, way in enumerate(ways):
-
-        @pl.when(way < 0)
-        def _():
-            held_ref[slot] = jnp.zeros_like(held_ref[slot])
-
-    bring(lambda copy: copy.wait())
-    copy = pltpu.make_async_copy(held_ref, owned_ref, sem.at[CAP])
-    copy.start()
-    copy.wait()
-
-
-def begin(table, sources):
+
+            @pl.when(way < 0)
+            def _():
+                for i in range(owned_ref.shape[1] // tile):
+                    act(pltpu.make_async_copy(zero_ref, owned_ref.at[slot, pl.ds(i * tile, tile)], out_sem.at[slot, i]))
+
+    def own(act):
+        for slot, way in enumerate(ways):
+
+            @pl.when(way == 0)
+            def _():
+                act(pltpu.make_async_copy(held_ref, owned_ref.at[slot], out_sem.at[slot, 0]))
+
+    zeros(lambda copy: copy.start())
+    bring.wait()
+    own(lambda copy: copy.start())
+    zeros(lambda copy: copy.wait())
+    own(lambda copy: copy.wait())
+
+
+def begin(table, lists, mine):
     hbm = pl.BlockSpec(memory_space=pltpu.HBM)
-    shape = (CAP, *sources[0].shape)
+    rows, cols = mine.shape
+    tile = min(256, rows)
     return pl.pallas_call(
         begin_kernel,
         grid_spec=pltpu.PrefetchScalarGridSpec(
             num_scalar_prefetch=1,
             grid=(1,),
-            in_specs=[hbm] * len(sources),
+            in_specs=[pl.BlockSpec(lists.shape, lambda *_: (0, 0)), hbm],
+            out_specs=[hbm, pl.BlockSpec(lists.shape, lambda *_: (0, 0))],
+            scratch_shapes=[
+                pltpu.VMEM((rows, cols), mine.dtype),
+                pltpu.VMEM((tile, cols), mine.dtype),
+                pltpu.SemaphoreType.DMA,
+                pltpu.SemaphoreType.DMA((CAP, rows // tile)),
+            ],
+        ),
+        out_shape=[
+            jax.ShapeDtypeStruct((CAP, rows, cols), mine.dtype),
+            jax.ShapeDtypeStruct(lists.shape, lists.dtype),
+        ],
+        compiler_params=pltpu.CompilerParams(vmem_limit_bytes=8 * 1024 * 1024),
+        cost_estimate=pl.CostEstimate(flops=0, bytes_accessed=6 * rows * cols, transcendentals=0),
+        name="begin",
+    )(table, lists, mine)
+
+
+def receive_kernel(table_ref, *refs):
+    sources, (_, owned_ref, held_ref, in_sem, out_sem) = refs[:-5], refs[-5:]
+    plane, dp = lax.axis_index("owner"), lax.axis_index("dp")
+    parts = in_sem.shape[1]
+    rows = held_ref.shape[1] // parts
+    steps = [(slot, part) for slot in range(CAP) for part in range(parts)]
+    ways = [table_ref[WAYS + slot * PLANES + plane, dp] for slot in range(CAP)]
+
+    def bring(slot, part, act):
+        span = pl.ds(part * rows, rows)
+        for k, source in enumerate(sources):
+
+            @pl.when(ways[slot] == k + 1)
+            def _():
+                act(pltpu.make_async_copy(source.at[span], held_ref.at[slot, span], in_sem.at[slot, part]))
+
+    def put(slot, part, act):
+        span = pl.ds(part * rows, rows)
+
+        @pl.when(ways[slot] > 0)
+        def _():
+            act(pltpu.make_async_copy(held_ref.at[slot, span], owned_ref.at[slot, span], out_sem.at[slot, part]))
+
+    for step in steps:
+        bring(*step, lambda copy: copy.start())
+    for step in steps:
+        bring(*step, lambda copy: copy.wait())
+        put(*step, lambda copy: copy.start())
+    for step in steps:
+        put(*step, lambda copy: copy.wait())
+
+
+def receive(table, sources, owned):
+    hbm = pl.BlockSpec(memory_space=pltpu.HBM)
+    parts = 4
+    return pl.pallas_call(
+        receive_kernel,
+        grid_spec=pltpu.PrefetchScalarGridSpec(
+            num_scalar_prefetch=1,
+            grid=(1,),
+            in_specs=[hbm] * (len(sources) + 1),
             out_specs=hbm,
-            scratch_shapes=[pltpu.VMEM(shape, jnp.bfloat16), pltpu.SemaphoreType.DMA((CAP + 1,))],
+            scratch_shapes=[
+                pltpu.VMEM(owned.shape, owned.dtype),
+                pltpu.SemaphoreType.DMA((CAP, parts)),
+                pltpu.SemaphoreType.DMA((CAP, parts)),
+            ],
         ),
-        out_shape=jax.ShapeDtypeStruct(shape, jnp.bfloat16),
+        out_shape=jax.ShapeDtypeStruct(owned.shape, owned.dtype),
+        input_output_aliases={1 + len(sources): 0},
         compiler_params=pltpu.CompilerParams(vmem_limit_bytes=8 * 1024 * 1024),
-        cost_estimate=pl.CostEstimate(flops=0, bytes_accessed=4 * math.prod(shape), transcendentals=0),
-        name="begin",
-    )(table, *sources)
+        name="receive",
+    )(table, *sources, owned)
 
 
 def finish_kernel(lists_ref, rows_ref, _, update_ref, owned_ref, staged_ref, sem):
@@ -464,7 +533,9 @@
     with jax.named_scope("return_rows"):
         arrived = lax.all_to_all(mine.reshape(devices, rows, cols), both, 0, 0, tiled=True)
     with jax.named_scope("owned"):
-        owned = begin(table, [mine, *(lax.ppermute(mine, "dp", step) for step in chip_steps())])
+        sources = [lax.ppermute(mine, "dp", step) for step in chip_steps()]
+        owned, lists = begin(table, lists, mine)
+        owned = receive(table, sources, owned)
 
     def with_left(owned, arrived):
         plane, dp = lax.axis_index("owner"), lax.axis_index("dp")

time: 127 us -> 126 us (level)
  waiting for transfers between devices: 34.9 us -> 32 us
  Pallas kernels: 19.5 us -> 21.7 us
    pallas_call x0 -> x1, Pallas kernels: none -> 3.33 us  [receive(): pl.pallas_call(receive_kernel, grid_spec=pltpu.PrefetchScalarGridSpec(num...]
    all_to_all x1, waiting for transfers between devices: 4.26 us -> 2.41 us  [shards(): lax.all_to_all(mine.reshape(devices, rows, cols), both, 0, 0, tiled=True)]
  transfers between devices with their start and end apart: 4 -> 4, of which waited for: 2 -> 3; matrix products, arithmetic and copies ran while one was open for 0% -> 0% of each run, Pallas kernels for 2% -> 5%
where the time goes in v2:
time: 126 us; the launch traced here: 124 us
  blocking collectives  56.5 us (45%)
  waiting for transfers between devices  32 us (25%)
  Pallas kernels  21.7 us (17%)
  starting transfers between devices  10.5 us (8%)
  local copies, waits for them, and re-layouts  2.27 us (2%)
  between operations  1.5 us (1%)
    all_to_all x1, blocking collectives, shards(): received = lax.all_to_all(outgoing, both, 0, 0, tiled=True)  56.5 us
    ppermute x3, waiting for transfers between devices, shards(): sources = [lax.ppermute(mine, 'dp', step) for step in chip_steps()]  29.5 us
    pallas_call x1, Pallas kernels, start(): pl.pallas_call(functools.partial(start_kernel, planes), grid=(1,), in_spe...  7.62 us
    all_to_all x1, starting transfers between devices, shards(): lax.all_to_all(mine.reshape(devices, rows, cols), both, 0, 0, tiled=True)  7.3 us
    pallas_call x1, Pallas kernels, orthogonalize(): pl.pallas_call(functools.partial(orthogonalize_kernel, scale), out_shape=...  6.02 us
    pallas_call x1, Pallas kernels, receive(): pl.pallas_call(receive_kernel, grid_spec=pltpu.PrefetchScalarGridSpec(num...  3.33 us
    ppermute x3, starting transfers between devices, shards(): sources = [lax.ppermute(mine, 'dp', step) for step in chip_steps()]  3.25 us
  transfers between devices with their start and end apart: 4, of which 3 were waited for; matrix products, arithmetic and copies ran while one was open for 0% of the time, Pallas kernels for 5%

profile of v2, /device:TPU:34, one launch (start us, length us, event | category | flops | bytes accessed | tf_op | source)
XLA Modules:
  0.0 124.4 jit_solution(4212281069446670310)
XLA Ops:
  0.6 7.6 %start.1 = (s32[56,128]{1,0:T(8,128)S(1)}, s32[8,256]{1,0:T(8,128)}, f32[192,4,768]{2,1,0:T(4,128)}, bf16[256,4,768]{2,1,0:T(4,128)(2,1)}) custom-call(s32[1,192]{1,0:T(1,128)} %bitcast.7, f32[192,4,768]{2,1,0:T(4,128)} %momentum_ref.1, bf16[192,4,768]{2,1,0:T(4,128)(2,1)} %grad_ref.1), custom_call_target="tpu_custom_call" | custom-call | tf_op jit(solution)/shard_map/start/start/pallas_call | solution.py:254
  8.3 56.5 %all_to_all.18 = bf16[256,4,768]{2,1,0:T(4,128)(2,1)S(1)} all-to-all(bf16[256,4,768]{2,1,0:T(4,128)(2,1)} %get-tuple-element.24), channel_id=1, replica_groups=mesh['dp'=32,'owner'=8] {'dp','owner'}, dimensions={0} | all-to-all | bytes 3145728 | tf_op jit(solution)/shard_map/gather_matrix/all_to_all | solution.py:529
  64.8 0.4 reshape.52.x_ref
  65.2 6.0 %orthogonalize.1.mine_ref = bf16[1024,768]{1,0:T(8,128)(2,1)S(1)} custom-call(bf16[1024,768]{1,0:T(8,128)(2,1)S(1)} %reshape.52.x_ref), custom_call_target="tpu_custom_call" | custom-call | flops 6643777536 | bytes 3145728 | tf_op jit(solution)/shard_map/orthogonalize/orthogonalize/pallas_call | solution.py:330
  71.2 1.3 %reshape.53 = bf16[256,4,768]{2,1,0:T(4,128)(2,1)} reshape(bf16[1024,768]{1,0:T(8,128)(2,1)S(1)} %orthogonalize.1.mine_ref) | data formatting | bytes 3145728 | tf_op jit(solution)/shard_map/return_rows/reshape | solution.py:534
  72.5 0.0 copy-start
  72.5 7.3 %all-to-all-start.3 = ((bf16[256,4,768]{2,1,0:T(4,128)(2,1)}), bf16[256,4,768]{2,1,0:T(4,128)(2,1)S(1)}, u32[]{:S(2)}, u32[]{:S(2)}) async-start(bf16[256,4,768]{2,1,0:T(4,128)(2,1)} %reshape.53), calls=%async_computation.3 | async-start | bytes 3145728 | tf_op jit(solution)/shard_map/return_rows/all_to_all | solution.py:534
  79.8 0.2 collective-permute-start
  80.1 1.5 %collective-permute-start.1 = (bf16[1024,768]{1,0:T(8,128)(2,1)S(1)}, bf16[1024,768]{1,0:T(8,128)(2,1)S(1)}, u32[]{:S(2)}, u32[]{:S(2)}) collective-permute-start(bf16[1024,768]{1,0:T(8,128)(2,1)S(1)} %orthogonalize.1.mine_ref), channel_id=1, source_target_pairs={{0,64},{8,200},{16,80},{24,216},{32,96},{40,232},{48,112},{56,248}... | collective-permute-start | bytes 4718600 | tf_op jit(solution)/shard_map/owned/ppermute | solution.py:536
  81.5 1.5 %collective-permute-start.2 = (bf16[1024,768]{1,0:T(8,128)(2,1)S(1)}, bf16[1024,768]{1,0:T(8,128)(2,1)S(1)}, u32[]{:S(2)}, u32[]{:S(2)}) collective-permute-start(bf16[1024,768]{1,0:T(8,128)(2,1)S(1)} %orthogonalize.1.mine_ref), channel_id=1, source_target_pairs={{0,16},{8,56},{16,32},{24,8},{32,48},{40,24},{48,0},{56,40},{64,80... | collective-permute-start | bytes 4718600 | tf_op jit(solution)/shard_map/owned/ppermute | solution.py:536
  83.1 0.5 slice.3
  84.3 0.0 copy-done
  84.3 2.4 %begin.1 = (bf16[2,1024,768]{2,1,0:T(8,128)(2,1)}, s32[8,256]{1,0:T(8,128)S(1)}) custom-call(s32[56,128]{1,0:T(8,128)S(1)} %get-tuple-element.22.table_ref, s32[8,256]{1,0:T(8,128)S(1)} %copy-done, bf16[1024,768]{1,0:T(8,128)(2,1)S(1)} %orthogonalize.1.mine_ref), custom_call_target="tpu_custom_call" | custom-call | bytes 4718592 | tf_op jit(solution)/shard_map/owned/begin/pallas_call | solution.py:379
  86.6 0.0 collective-permute-done.refs_0_
  86.7 26.1 %collective-permute-done.1.refs_1_ = bf16[1024,768]{1,0:T(8,128)(2,1)S(1)} collective-permute-done((bf16[1024,768]{1,0:T(8,128)(2,1)S(1)}, bf16[1024,768]{1,0:T(8,128)(2,1)S(1)}, u32[]{:S(2)}, u32[]{:S(2)}) %collective-permute-start.1) | collective-permute-done | bytes 1572896 | tf_op jit(solution)/shard_map/owned/ppermute | solution.py:536
  112.8 3.4 %collective-permute-done.2.refs_2_ = bf16[1024,768]{1,0:T(8,128)(2,1)S(1)} collective-permute-done((bf16[1024,768]{1,0:T(8,128)(2,1)S(1)}, bf16[1024,768]{1,0:T(8,128)(2,1)S(1)}, u32[]{:S(2)}, u32[]{:S(2)}) %collective-permute-start.2) | collective-permute-done | bytes 1572896 | tf_op jit(solution)/shard_map/owned/ppermute | solution.py:536
  116.2 3.3 %receive.1 = bf16[2,1024,768]{2,1,0:T(8,128)(2,1)} custom-call(s32[56,128]{1,0:T(8,128)S(1)} %get-tuple-element.22.table_ref, bf16[1024,768]{1,0:T(8,128)(2,1)S(1)} %collective-permute-done.refs_0_, bf16[1024,768]{1,0:T(8,128)(2,1)S(1)} %collective-permute-done.1.refs_1_, ...), custom_call_target="tpu_custom_call", output_to_operand_aliasing={{}: (4, {})} | custom-call | tf_op jit(solution)/shard_map/owned/receive/pallas_call | solution.py:438
  119.5 2.4 %all-to-all-done.3.rows_ref = bf16[256,4,768]{2,1,0:T(4,128)(2,1)S(1)} async-done(((bf16[256,4,768]{2,1,0:T(4,128)(2,1)}), bf16[256,4,768]{2,1,0:T(4,128)(2,1)S(1)}, u32[]{:S(2)}, u32[]{:S(2)}) %all-to-all-start.3) | async-done | bytes 1572896 | tf_op jit(solution)/shard_map/return_rows/all_to_all | solution.py:534
  121.9 2.3 %finish.1 = (f32[192,4,768]{2,1,0:T(4,128)}, bf16[2,1024,768]{2,1,0:T(8,128)(2,1)}) custom-call(s32[8,256]{1,0:T(8,128)S(1)} %get-tuple-element.25.lists_ref, bf16[256,4,768]{2,1,0:T(4,128)(2,1)S(1)} %all-to-all-done.3.rows_ref, bf16[2,1024,768]{2,1,0:T(8,128)(2,1)} %get-tuple-element.32._), custom_call_target="tpu_custom_call", output_to_operand_aliasing={{1}: (2, {})} | custom-call | tf_op jit(solution)/shard_map/finish/finish/pallas_call | solution.py:479
  (1 shorter events, 0.0 us)
Async XLA Ops:
  72.5 11.7 %copy-start = (s32[8,256]{1,0:T(8,128)S(1)}, s32[8,256]{1,0:T(8,128)}, u32[]{:S(2)}) copy-start(s32[8,256]{1,0:T(8,128)} %get-tuple-element.23.lists_ref) | copy-start | bytes 24580
  72.5 49.4 %all-to-all-start.3 = ((bf16[256,4,768]{2,1,0:T(4,128)(2,1)}), bf16[256,4,768]{2,1,0:T(4,128)(2,1)S(1)}, u32[]{:S(2)}, u32[]{:S(2)}) async-start(bf16[256,4,768]{2,1,0:T(4,128)(2,1)} %reshape.53), calls=%async_computation.3 | async-start | bytes 3145728 | tf_op jit(solution)/shard_map/return_rows/all_to_all | solution.py:534
  79.8 6.8 %collective-permute-start = (bf16[1024,768]{1,0:T(8,128)(2,1)S(1)}, bf16[1024,768]{1,0:T(8,128)(2,1)S(1)}, u32[]{:S(2)}, u32[]{:S(2)}) collective-permute-start(bf16[1024,768]{1,0:T(8,128)(2,1)S(1)} %orthogonalize.1.mine_ref), channel_id=1, source_target_pairs={{0,8},{8,0},{16,24},{24,16},{32,40},{40,32},{48,56},{56,48},{64,72... | collective-permute-start | bytes 4718600 | tf_op jit(solution)/shard_map/owned/ppermute | solution.py:536
  80.1 32.7 %collective-permute-start.1 = (bf16[1024,768]{1,0:T(8,128)(2,1)S(1)}, bf16[1024,768]{1,0:T(8,128)(2,1)S(1)}, u32[]{:S(2)}, u32[]{:S(2)}) collective-permute-start(bf16[1024,768]{1,0:T(8,128)(2,1)S(1)} %orthogonalize.1.mine_ref), channel_id=1, source_target_pairs={{0,64},{8,200},{16,80},{24,216},{32,96},{40,232},{48,112},{56,248}... | collective-permute-start | bytes 4718600 | tf_op jit(solution)/shard_map/owned/ppermute | solution.py:536
  81.5 34.7 %collective-permute-start.2 = (bf16[1024,768]{1,0:T(8,128)(2,1)S(1)}, bf16[1024,768]{1,0:T(8,128)(2,1)S(1)}, u32[]{:S(2)}, u32[]{:S(2)}) collective-permute-start(bf16[1024,768]{1,0:T(8,128)(2,1)S(1)} %orthogonalize.1.mine_ref), channel_id=1, source_target_pairs={{0,16},{8,56},{16,32},{24,8},{32,48},{40,24},{48,0},{56,40},{64,80... | collective-permute-start | bytes 4718600 | tf_op jit(solution)/shard_map/owned/ppermute | solution.py:536
